TPU v7x, 256 devices: a whole 4x4x8 slice. The times are simulated.
256 devices in a mesh: rep: 4 (over z_lo, core), fsdp: 64 (over z_hi, y, x).
Axes of the slice: x: 4, y: 4, z: 8 (z_hi: 4, z_lo: 2; z = z_hi * 2 + z_lo), core: 2. Of those that a mesh axis runs over, the one named last changes fastest.
Arguments:
- activations: bfloat16 [196608, 8192], P(('rep', 'fsdp')), may hold values from -24 to 24
- cotangents: bfloat16 [196608, 512], P(('rep', 'fsdp')), may hold values from -6 to 6
- momentum: float32 [4, 8192, 512], P('rep', 'fsdp'), may hold values from -6 to 6
Outputs:
- update: float32 [8192, 512], P('fsdp')
- new_momentum: float32 [4, 8192, 512], P('rep', 'fsdp')
All inputs are finite; a program needn't handle non-finite values.
Results may differ from a plain program's by a relative error of at most 0.0003.
Values may be sent and summed in bfloat16 or wider, within the bound.
A program may use at most 192 MiB of HBM per device.

v0:
```python
import math

import jax
import jax.numpy as jnp
from jax import lax
from jax.sharding import PartitionSpec as P


def dct_basis():
    wavenum = jnp.arange(16, dtype=jnp.float32)[:, None]
    sample_pos = jnp.arange(64, dtype=jnp.float32)[None, :]
    factor = jnp.where(wavenum == 0, math.sqrt(1.0 / 64.0), math.sqrt(2.0 / 64.0))
    return factor * jnp.cos(math.pi * (2.0 * sample_pos + 1.0) * wavenum / 128.0)


def band_of(field, basis):
    rows, cols = field.shape
    blocks = field.reshape(rows // 64, 64, cols // 64, 64)
    coeffs = jnp.einsum("fs,asbt,gt->afbg", basis, blocks, basis, precision=lax.Precision.HIGHEST)
    return coeffs.reshape(rows // 4, cols // 4)


def spread_band(band, basis):
    rows, cols = band.shape
    blocks = band.reshape(rows // 16, 16, cols // 16, 16)
    values = jnp.einsum("fs,afbg,gt->asbt", basis, blocks, basis, precision=lax.Precision.HIGHEST)
    return values.reshape(rows * 4, cols * 4)


def shards(activations, cotangents, momentum):
    basis = dct_basis()
    group_tok = activations.shape[0] * lax.axis_size("fsdp")
    gradient = lax.psum_scatter(
        lax.dot_general(
            activations, cotangents, (((0,), (0,)), ((), ())), preferred_element_type=jnp.float32
        ),
        "fsdp",
        scatter_dimension=0,
        tiled=True,
    )
    gradient = gradient / math.sqrt(group_tok)
    accum = 0.9 * momentum[0] + gradient
    own_band = band_of(accum, basis)
    every_band = lax.all_gather(own_band[None], "rep", axis=0, tiled=True)
    mean_band = jnp.mean(every_band, axis=0)
    update = spread_band(mean_band, basis)
    new_momentum = (accum - spread_band(own_band, basis))[None]
    return (update, new_momentum)


def solution(mesh):
    return jax.shard_map(
        shards,
        mesh=mesh,
        in_specs=(P(("rep", "fsdp"), None), P(("rep", "fsdp"), None), P("rep", "fsdp", None)),
        out_specs=(P("fsdp", None), P("rep", "fsdp", None)),
        check_vma=False,
    )
```

profile of v0, /device:TPU:1, one launch (start us, length us, event | category | flops | bytes accessed | tf_op | source)
XLA Modules:
  0.0 475.7 jit_solution(11667614816529155965)
XLA Ops:
  7.2 0.0 copy-start
  7.2 0.0 reduce-scatter.2.cloned.1.call-start
  7.2 1.1 copy-done
  8.3 15.0 %fusion.35 = f32[8192,512]{1,0:T(8,128)} fusion(bf16[768,8192]{1,0:T(8,128)(2,1)} %param.3, bf16[768,512]{1,0:T(8,128)(2,1)S(1)} %copy-done), kind=kOutput, calls=%fused_computation.44 | convolution fusion | flops 6442450944 | bytes 30146560 | tf_op jit(solution)/shard_map/dot_general | solution.py:34
  23.3 0.0 copy-start.1
  23.3 0.0 reduce-scatter.2.cloned.1.call-update
  23.3 418.9 %reduce-scatter.2.cloned.1.call-done = f32[128,512]{1,0:T(8,128)} async-done(((f32[8192,512]{1,0:T(8,128)}), f32[128,512]{1,0:T(8,128)}) %reduce-scatter.2.cloned.1.call-update) | async-done | bytes 262160 | tf_op jit(solution)/shard_map/reduce_scatter | solution.py:33
  442.2 0.0 copy-done.1
  442.2 1.0 bitcast_add_fusion
  443.2 0.1 reshape.35
  443.4 0.5 fusion
  443.8 0.3 convolution_bitcast_fusion.2
  444.2 0.4 fusion.5
  444.6 0.1 broadcast_in_dim_reshape.3
  444.7 19.2 %all_gather.3 = f32[4,32,128]{2,1,0:T(8,128)S(1)} all-gather(f32[1,32,128]{2,1,0:T(8,128)S(1)} %broadcast_in_dim_reshape.3), channel_id=1, replica_groups=mesh['rep'=4,'fsdp'=64] {'rep'}, dimensions={0}, use_global_device_ids=true | all-gather | bytes 81920 | tf_op jit(solution)/shard_map/all_gather | solution.py:44
  463.9 0.1 div.36
  464.0 0.4 fusion.2
  464.4 1.0 convolution_bitcast_fusion.1
  465.5 0.3 copy.17
  465.8 0.9 reshape.36
  466.7 1.0 convolution_bitcast_fusion
  467.7 0.3 copy.19
  468.0 0.1 reshape.37
  468.2 0.7 subtract_bitcast_fusion
  (5 shorter events, 0.1 us)
Async XLA Ops:
  7.2 1.1 copy-start
  7.2 435.0 %reduce-scatter.2.cloned.1.call-start = ((), (), s32[]{:S(2)}) async-start(), calls=%async_computation.1 | async-start | bytes 17039360 | tf_op jit(solution)/shard_map/reduce_scatter | solution.py:33
  23.3 418.9 %copy-start.1 = (f32[1,128,512]{2,1,0:T(8,128)S(1)}, f32[1,128,512]{2,1,0:T(8,128)}, u32[]{:S(2)}) copy-start(f32[1,128,512]{2,1,0:T(8,128)} %param.5) | copy-start | bytes 786436
Sparse Core Ops, SparseCore 0:
  23.4 418.7 reduce-scatter.1
where the time goes:
time: 476 us
  waiting for transfers between devices  419 us (88%)
  blocking collectives  19.2 us (4%)
  matrix products  18.6 us (4%)
  between operations  14.1 us (3%)
    reduce_scatter x1, waiting for transfers between devices, shards(): lax.psum_scatter(lax.dot_general(activations, cotangents, (((0,), (0,)),...  419 us
    all_gather x1, blocking collectives, shards(): every_band = lax.all_gather(own_band[None], 'rep', axis=0, tiled=True)  19.2 us
    dot_general x1, matrix products, shards(): lax.dot_general(activations, cotangents, (((0,), (0,)), ((), ())), prefer...  15 us
  transfers between devices with their start and end apart: 1, of which 1 were waited for; matrix products, arithmetic and copies ran while one was open for 0% of the time, Pallas kernels for 0%

commit v1 on v0

v1 whole, which is shorter than its diff:
```python
import functools
import math

import jax
import jax.numpy as jnp
import numpy as np
from jax import lax
from jax.experimental import pallas as pl
from jax.experimental.pallas import tpu as pltpu
from jax.sharding import PartitionSpec as P

F32 = jnp.float32
BF16 = jnp.bfloat16
FIRST = ((1, 2), (3, 2))
NEXT = (3, 1)
SLABS = (2, 1, 3, 0)
SPAN = 250.0


def dct_basis():
    wavenum = np.arange(16)[:, None]
    sample_pos = np.arange(64)[None, :]
    factor = np.where(wavenum == 0, math.sqrt(1.0 / 64.0), math.sqrt(2.0 / 64.0))
    return (factor * np.cos(math.pi * (2.0 * sample_pos + 1.0) * wavenum / 128.0)).astype(np.float32)


def flip(v, mask):
    return (v // 2 + mask // 2) % 2 * 2 + (v % 2 + mask % 2) % 2


def encode(v):
    size = jnp.abs(v)
    s = jnp.maximum(jnp.max(size, axis=0, keepdims=True), 1e-30)
    code = jnp.exp2(size * (SPAN / s) - SPAN / 2)
    return jnp.where(v < 0, -code, code).astype(BF16), s


def decode(code, s):
    code = code.astype(F32)
    size = jnp.log(jnp.abs(code)) * (s * (1.0 / (SPAN * math.log(2.0)))) + s * 0.5
    return jnp.where(code < 0, -size, size)


def kernel(
    group_tok, a_hbm, c_ref, mom_ref, left_ref, left_t_ref, right_ref, right_t_ref, up_ref, new_ref,
    a, ct, pt, s1, s2, s3, s4, s5, s6, r1, r2, r3, r4, r5, r6, ssc, rsc, band, bands,
    a_sem, ss, rs, sss, rss, band_ss, band_rs,
):
    rep, own = lax.axis_index("rep"), lax.axis_index("fsdp")
    z0, y0, x0 = own // 16, own // 4 % 4, own % 4
    sends, recvs = (s1, s2, s3, s4, s5, s6), (r1, r2, r3, r4, r5, r6)

    def partner(axis, mask):
        z, y, x = z0, y0, x0
        if axis == "x":
            x = flip(x, mask)
        elif axis == "y":
            y = flip(y, mask)
        else:
            z = flip(z, mask)
        return (rep, z * 16 + y * 4 + x)

    def block_copy(q, zh):
        first = pl.multiple_of((zh * 16 + flip(y0, q) * 4) * 128, 512)
        cols = pl.ds(first, 512)
        return pltpu.make_async_copy(a_hbm.at[:, cols], a.at[:, cols], a_sem.at[q, zh])

    for q in SLABS:
        for zh in range(4):
            block_copy(q, zh).start()

    barrier = pltpu.get_barrier_semaphore()
    others = [partner(axis, mask) for axis in "xyz" for mask in (1, 3)]
    others += [((rep + i) % 4, own) for i in (1, 2, 3)]
    for other in others:
        pl.semaphore_signal(barrier, inc=1, device_id=other)
    ct[...] = c_ref[...].T
    pl.semaphore_wait(barrier, len(others))

    def axis_of(f, stage):
        return ("xxzzyy", "yyzzxx")[f][stage]

    def mask_of(p, stage):
        return (FIRST[p][0], NEXT[p])[stage % 2]

    def data(f, p, q, stage, part=None):
        src, dst = sends[stage].at[f, p, q], recvs[stage].at[f, p, q]
        if part is not None:
            src, dst = src.at[part], dst.at[part]
        return pltpu.make_async_remote_copy(
            src, dst, ss.at[f, p, q, stage], rs.at[f, p, q, stage],
            device_id=partner(axis_of(f, stage), mask_of(p, stage)),
        )

    def scales(f, p, q, stage):
        return pltpu.make_async_remote_copy(
            ssc.at[f, p, q, stage], rsc.at[f, p, q, stage], sss.at[f, p, q, stage], rss.at[f, p, q, stage],
            device_id=partner(axis_of(f, stage), mask_of(p, stage)),
        )

    def wait_recv(f, p, q, stage):
        data(f, p, q, stage).wait_recv()
        scales(f, p, q, stage).wait_recv()

    def put(f, p, q, stage, at, row, v):
        code, s = encode(v)
        sends[stage][(f, p, q) + at] = code
        ssc[f, p, q, stage, pl.ds(row, 1), :] = s

    def got(f, p, q, stage, at, row):
        return decode(recvs[stage][(f, p, q) + at], rsc[f, p, q, stage, pl.ds(row, 1), :])

    def rows(p):
        return slice(p * 128, p * 128 + 128)

    def multiply(f, q):
        def one(rz, carry):
            zh = flip(z0, rz)
            parts = []
            for r in range(4):
                y, x = (flip(y0, q), flip(x0, r)) if f == 0 else (flip(y0, r), flip(x0, q))
                parts.append(a[:, pl.ds(pl.multiple_of((zh * 16 + y * 4 + x) * 128, 128), 128)])
            total = jnp.dot(ct[f * 256 : f * 256 + 256, :], jnp.concatenate(parts, axis=1), preferred_element_type=F32)
            for r in range(4):
                pt[f, q, rz, r] = total[:, r * 128 : r * 128 + 128]
            for p in range(2):
                for j, r in enumerate(FIRST[p]):
                    put(f, p, q, 0, (rz, j), rz * 2 + j, pt[f, q, rz, r, rows(p), :])
                data(f, p, q, 0, rz).start()
            return carry

        lax.fori_loop(0, 4, one, 0)
        for p in range(2):
            scales(f, p, q, 0).start()

    def second(f, q):
        for p in range(2):
            wait_recv(f, p, q, 0)

            def one(rz, carry):
                v = pt[f, q, rz, NEXT[p], rows(p), :] + got(f, p, q, 0, (rz, 1), rz * 2 + 1)
                put(f, p, q, 1, (rz,), rz, v)
                data(f, p, q, 1, rz).start()
                pt[f, q, rz, 0, rows(p), :] += got(f, p, q, 0, (rz, 0), rz * 2)
                return carry

            lax.fori_loop(0, 4, one, 0)
            scales(f, p, q, 1).start()

    def third(f, q):
        for p in range(2):
            wait_recv(f, p, q, 1)
            for j, rz in enumerate(FIRST[p]):
                put(f, p, q, 2, (j,), j, pt[f, q, rz, 0, rows(p), :] + got(f, p, q, 1, (rz,), rz))
            data(f, p, q, 2).start()
            scales(f, p, q, 2).start()
            for rz in (0, NEXT[p]):
                pt[f, q, rz, 0, rows(p), :] += got(f, p, q, 1, (rz,), rz)

    def fourth(f, q):
        for p in range(2):
            wait_recv(f, p, q, 2)
            put(f, p, q, 3, (), 0, pt[f, q, NEXT[p], 0, rows(p), :] + got(f, p, q, 2, (1,), 1))
            data(f, p, q, 3).start()
            scales(f, p, q, 3).start()
            pt[f, q, 0, 0, rows(p), :] += got(f, p, q, 2, (0,), 0)

    def fifth(f, q):
        for p in range(2):
            wait_recv(f, p, q, 3)
            v = pt[f, q, 0, 0, rows(p), :] + got(f, p, q, 3, (), 0)
            if q in FIRST[p]:
                j = FIRST[p].index(q)
                put(f, p, j, 4, (), 0, v)
                data(f, p, j, 4).start()
                scales(f, p, j, 4).start()
            else:
                pt[f, q, 0, 0, rows(p), :] = v

    def sixth(f):
        for p in range(2):
            wait_recv(f, p, 1, 4)
            put(f, p, 0, 5, (), 0, pt[f, NEXT[p], 0, 0, rows(p), :] + got(f, p, 1, 4, (), 0))
            data(f, p, 0, 5).start()
            scales(f, p, 0, 5).start()

    def last(f):
        for p in range(2):
            wait_recv(f, p, 0, 4)
            wait_recv(f, p, 0, 5)
            pt[f, 0, 0, 0, rows(p), :] += got(f, p, 0, 4, (), 0) + got(f, p, 0, 5, (), 0)

    steps = [multiply, second, third, fourth, fifth]
    for t in range(4 + len(steps) - 1):
        for k in range(len(steps)):
            if 0 <= t - k < 4:
                for f in range(2):
                    if k == 0 and (f == 0 or t == 0):
                        for q in [SLABS[t]] if f == 0 else SLABS[1:]:
                            if f == 0 and t > 0:
                                continue
                            for zh in range(4):
                                block_copy(q, zh).wait()
                    steps[k](f, SLABS[t - k])
    for f in range(2):
        sixth(f)
    for f in range(2):
        last(f)

    def exact(l, r):
        return jnp.dot(l, r, preferred_element_type=F32, precision=lax.Precision.HIGHEST)

    total = jnp.concatenate([pt[f, 0, 0, 0] for f in range(2)], axis=0)
    accum = 0.9 * mom_ref[0] + total.T * (1.0 / math.sqrt(group_tok))
    mine = exact(exact(left_ref[...], accum), right_ref[...])
    band[...] = mine
    copies = [
        pltpu.make_async_remote_copy(
            band, bands.at[i - 1], band_ss.at[i - 1], band_rs.at[i - 1], device_id=((rep + i) % 4, own)
        )
        for i in (1, 2, 3)
    ]
    for copy in copies:
        copy.start()
    new_ref[0] = accum - exact(exact(left_t_ref[...], mine), right_t_ref[...])
    for copy in copies:
        copy.wait_recv()
    mean = (mine + bands[0] + bands[1] + bands[2]) * 0.25
    up_ref[...] = exact(exact(left_t_ref[...], mean), right_t_ref[...])
    for copy in copies:
        copy.wait_send()
    for f in range(2):
        for p in range(2):
            for stage, slabs in enumerate((4, 4, 4, 4, 2, 1)):
                for q in range(slabs):
                    data(f, p, q, stage).wait_send()
                    scales(f, p, q, stage).wait_send()


def shards(activations, cotangents, momentum):
    tok, d = activations.shape
    kw = cotangents.shape[1]
    basis = dct_basis()
    left = np.kron(np.eye(2, dtype=np.float32), basis)
    right = np.kron(np.eye(kw // 64, dtype=np.float32), basis.T)
    constants = [jnp.asarray(m) for m in (left, left.T.copy(), right, right.T.copy())]
    counts = ((4, 4, 2), (4, 4), (4, 2), (4,), (2,), (1,))
    buffers = [pltpu.VMEM((2, 2) + n + (128, 128), BF16) for n in counts]
    vmem = pl.BlockSpec(memory_space=pltpu.VMEM)
    dma = pltpu.SemaphoreType.DMA
    return pl.pallas_call(
        functools.partial(kernel, tok * lax.axis_size("fsdp")),
        out_shape=(
            jax.ShapeDtypeStruct((128, kw), F32),
            jax.ShapeDtypeStruct((1, 128, kw), F32),
        ),
        in_specs=[pl.BlockSpec(memory_space=pl.ANY)] + [vmem] * 6,
        out_specs=(vmem, vmem),
        scratch_shapes=[
            pltpu.VMEM((tok, d), BF16),
            pltpu.VMEM((kw, tok), BF16),
            pltpu.VMEM((2, 4, 4, 4, 256, 128), F32),
            *buffers,
            *buffers,
            pltpu.VMEM((2, 2, 4, 6, 8, 128), F32),
            pltpu.VMEM((2, 2, 4, 6, 8, 128), F32),
            pltpu.VMEM((32, 128), F32),
            pltpu.VMEM((3, 32, 128), F32),
            dma((4, 4)),
            dma((2, 2, 4, 6)),
            dma((2, 2, 4, 6)),
            dma((2, 2, 4, 6)),
            dma((2, 2, 4, 6)),
            dma((3,)),
            dma((3,)),
        ],
        compiler_params=pltpu.CompilerParams(
            collective_id=0, has_side_effects=True, vmem_limit_bytes=60 * 2**20
        ),
        cost_estimate=pl.CostEstimate(flops=2 * tok * d * kw, bytes_accessed=2 * tok * (d + kw), transcendentals=0),
    )(activations, cotangents, momentum, *constants)


def solution(mesh):
    return jax.shard_map(
        shards,
        mesh=mesh,
        in_specs=(P(("rep", "fsdp"), None), P(("rep", "fsdp"), None), P("rep", "fsdp", None)),
        out_specs=(P("fsdp", None), P("rep", "fsdp", None)),
        check_vma=False,
    )
```

time: 476 us -> 87.8 us (0.18)
  waiting for transfers between devices: 419 us -> 0 us
  Pallas kernels: 0 us -> 83.7 us
  blocking collectives: 19.2 us -> 0 us
  matrix products: 18.6 us -> 0 us
  between operations: 14.1 us -> 0.64 us
    reduce_scatter x1 -> x0, waiting for transfers between devices: 419 us -> none  [shards(): lax.psum_scatter(lax.dot_general(activations, cotangents, (((0,), (0,)),...]
    pallas_call x0 -> x1, Pallas kernels: none -> 83.7 us  [shards(): pl.pallas_call(functools.partial(kernel, tok * lax.axis_size('fsdp')), ou...]
    all_gather x1 -> x0, blocking collectives: 19.2 us -> none  [shards(): every_band = lax.all_gather(own_band[None], 'rep', axis=0, tiled=True)]
    dot_general x7 -> x0, matrix products: 18.6 us -> none  [the longest x1 15 us: shards(): lax.dot_general(activations, cotangents, (((0,), (0,)), ((), ())), prefer...]
  transfers between devices with their start and end apart: 1 -> 0, of which waited for: 1 -> 0; matrix products, arithmetic and copies ran while one was open for 0% -> 0% of each run, Pallas kernels for 0% -> 0%
where the time goes in v1:
time: 87.8 us; the launch traced here: 87.7 us
  Pallas kernels  83.7 us (95%)
  local copies, waits for them, and re-layouts  3.34 us (4%)
    pallas_call x1, Pallas kernels, shards(): pl.pallas_call(functools.partial(kernel, tok * lax.axis_size('fsdp')), ou...  83.7 us
    unnamed x2, local copies, waits for them, and re-layouts  3.34 us

profile of v1, /device:TPU:1, one launch (start us, length us, event | category | flops | bytes accessed | tf_op | source)
XLA Modules:
  0.0 87.7 jit_solution(4298788985098008587)
XLA Ops:
  0.6 83.7 %shard_map.86 = (f32[128,512]{1,0:T(8,128)}, f32[1,128,512]{2,1,0:T(8,128)}) custom-call(bf16[768,8192]{1,0:T(8,128)(2,1)} %a_hbm.1, bf16[768,512]{1,0:T(8,128)(2,1)} %c_ref.1, f32[1,128,512]{2,1,0:T(8,128)} %mom_ref.1, f32[32,128]{1,0:T(8,128)} %constant.8.clone.left_ref, f32[128,32]{1,0:T(8,128)} %constant.9.clone.left_t_ref, ...), custom_call_target="tpu_custom_call" | custom-call | flops 6442450944 | bytes 13369344 | tf_op jit(solution)/shard_map/pallas_call | solution.py:251
  84.3 1.7 %copy.11 = f32[128,512]{1,0:T(8,128)} copy(f32[128,512]{1,0:T(8,128)} %get-tuple-element.4) | data formatting | bytes 524288
  86.0 1.7 %copy.12 = f32[1,128,512]{2,1,0:T(8,128)} copy(f32[1,128,512]{2,1,0:T(8,128)} %get-tuple-element.5) | data formatting | bytes 524288

commit v2 on v0

v2 whole, which is shorter than its diff:
```python
import functools
import math

import jax
import jax.numpy as jnp
import numpy as np
from jax import lax
from jax.experimental import pallas as pl
from jax.experimental.pallas import tpu as pltpu
from jax.sharding import PartitionSpec as P

F32 = jnp.float32
BF16 = jnp.bfloat16
FIRST = ((1, 2), (3, 2))
NEXT = (3, 1)
SLABS = (2, 1, 3, 0)
UNITS = (8, 4, 2, 1, 1, 1)
COUNTS = (4, 4, 4, 4, 2, 1)
SIZES = tuple(n * 128 + 16 for n in UNITS)
STARTS = tuple(sum(n * m for n, m in zip(SIZES[:i], COUNTS)) for i in range(7))
SPAN = 250.0


def dct_basis():
    wavenum = np.arange(16)[:, None]
    sample_pos = np.arange(64)[None, :]
    factor = np.where(wavenum == 0, math.sqrt(1.0 / 64.0), math.sqrt(2.0 / 64.0))
    return (factor * np.cos(math.pi * (2.0 * sample_pos + 1.0) * wavenum / 128.0)).astype(np.float32)


def flip(v, mask):
    return (v // 2 + mask // 2) % 2 * 2 + (v % 2 + mask % 2) % 2


def encode(v):
    size = jnp.abs(v)
    s = jnp.maximum(jnp.max(size, axis=0, keepdims=True), 1e-30)
    s = (s * 1.004).astype(BF16).astype(F32)
    code = jnp.exp2(size * (SPAN / s) - SPAN / 2)
    return jnp.where(v < 0, -code, code).astype(BF16), s


def decode(code, s):
    code = code.astype(F32)
    size = jnp.log(jnp.abs(code)) * (s * (1.0 / (SPAN * math.log(2.0)))) + s * 0.5
    return jnp.where(code < 0, -size, size)


def kernel(
    group_tok, a_hbm, c_hbm, mom_hbm, left_hbm, left_t_hbm, right_hbm, right_t_hbm, up_hbm, new_hbm,
    a, c, ct, mom, left, left_t, right, right_t, pt, sent, received, ssc, rsc, up, new, band, bands,
    a_sem, in_sem, out_sem, sent_sem, rs, band_ss, band_rs,
):
    rep, own = lax.axis_index("rep"), lax.axis_index("fsdp")
    z0, y0, x0 = own // 16, own // 4 % 4, own % 4

    def partner(axis, mask):
        z, y, x = z0, y0, x0
        if axis == "x":
            x = flip(x, mask)
        elif axis == "y":
            y = flip(y, mask)
        else:
            z = flip(z, mask)
        return (rep, z * 16 + y * 4 + x)

    def slab(t):
        return (t + 1) % 2 * 2 + (t + 1) // 2 % 2

    def block_copy(t, ry):
        first = pl.multiple_of((flip(z0, slab(t)) * 16 + flip(y0, ry) * 4) * 128, 512)
        cols = pl.ds(first, 512)
        return pltpu.make_async_copy(a_hbm.at[:, cols], a.at[:, cols], a_sem.at[t, ry])

    barrier = pltpu.get_barrier_semaphore()
    others = [partner(axis, mask) for axis in "xyz" for mask in (1, 3)]
    others += [((rep + i) % 4, own) for i in (1, 2, 3)]
    for other in others:
        pl.semaphore_signal(barrier, inc=1, device_id=other)
    pairs = [(c_hbm, c), (mom_hbm, mom), (left_hbm, left), (left_t_hbm, left_t), (right_hbm, right), (right_t_hbm, right_t)]
    inputs = [pltpu.make_async_copy(src, dst, in_sem.at[i]) for i, (src, dst) in enumerate(pairs)]
    inputs[0].start()
    for t in range(4):
        for ry in SLABS:
            block_copy(t, ry).start()
    for copy in inputs[1:]:
        copy.start()
    inputs[0].wait()
    ct[...] = c[...].T
    ssc[...] = jnp.zeros_like(ssc)

    def axis_of(f, stage):
        return ("xxyyzz", "yyxxzz")[f][stage]

    def mask_of(p, stage):
        return (FIRST[p][0], NEXT[p])[stage % 2]

    def begin(f, p, t, stage, row=0):
        at = (f * 2 + p) * STARTS[6] + STARTS[stage] + t * SIZES[stage] + row
        return at if isinstance(at, int) else pl.multiple_of(at, 16)

    def message(f, p, t, stage):
        where = pl.ds(begin(f, p, t, stage), SIZES[stage])
        return pltpu.make_async_remote_copy(
            sent.at[where], received.at[where], sent_sem.at[0], rs.at[f, p, t, stage],
            device_id=partner(axis_of(f, stage), mask_of(p, stage)),
        )

    def put(f, p, t, stage, row, v):
        code, s = encode(v)
        sent[pl.ds(begin(f, p, t, stage, row * 128), 128), :] = code
        ssc[f, p, pl.ds(row, 1), :] = s

    def send(f, p, t, stage):
        sent[pl.ds(begin(f, p, t, stage, UNITS[stage] * 128), 16), :] = ssc[f, p].astype(BF16)
        message(f, p, t, stage).start()

    def receive(f, p, t, stage):
        message(f, p, t, stage).wait_recv()
        rsc[f, p] = received[pl.ds(begin(f, p, t, stage, UNITS[stage] * 128), 16), :].astype(F32)

    def got(f, p, t, stage, row):
        return decode(received[pl.ds(begin(f, p, t, stage, row * 128), 128), :], rsc[f, p, pl.ds(row, 1), :])

    def unit(f, p, t, sec, pri):
        at = (sec, pri) if f == 0 else (pri, sec)
        return (t,) + at + (slice((f * 2 + p) * 128, (f * 2 + p) * 128 + 128), slice(None))

    def multiply(t, ry):
        zh = flip(z0, slab(t))
        block_copy(t, ry).wait()
        parts = []
        for rx in range(4):
            col = (zh * 16 + flip(y0, ry) * 4 + flip(x0, rx)) * 128
            parts.append(a[:, pl.ds(pl.multiple_of(col, 128), 128)])
        total = jnp.dot(ct[...], jnp.concatenate(parts, axis=1), preferred_element_type=F32)
        for rx in range(4):
            pt[t, ry, rx] = total[:, rx * 128 : rx * 128 + 128]

    def first(t):
        for ry in SLABS:
            multiply(t, ry)
            for p in range(2):
                for j, rx in enumerate(FIRST[p]):
                    put(0, p, t, 0, j * 4 + ry, pt[unit(0, p, t, ry, rx)])
            for p in range(2):
                if ry in FIRST[p]:
                    for rx in range(4):
                        put(1, p, t, 0, FIRST[p].index(ry) * 4 + rx, pt[unit(1, p, t, rx, ry)])
            if ry == 1:

                @pl.when(t == 0)
                def _():
                    pl.semaphore_wait(barrier, len(others))

                send(1, 0, t, 0)
            if ry == 3:
                send(1, 1, t, 0)
        send(0, 0, t, 0)
        send(0, 1, t, 0)

    def second(t):
        for f in (1, 0):
            for p in range(2):
                receive(f, p, t, 0)

                def one(sec, carry):
                    put(f, p, t, 1, sec, pt[unit(f, p, t, sec, NEXT[p])] + got(f, p, t, 0, 4 + sec))
                    pt[unit(f, p, t, sec, 0)] += got(f, p, t, 0, sec)
                    return carry

                lax.fori_loop(0, 4, one, 0)
                send(f, p, t, 1)

    def third(t):
        for f in (1, 0):
            for p in range(2):
                receive(f, p, t, 1)
                for j, sec in enumerate(FIRST[p]):
                    put(f, p, t, 2, j, pt[unit(f, p, t, sec, 0)] + got(f, p, t, 1, sec))
                send(f, p, t, 2)
                for sec in (0, NEXT[p]):
                    pt[unit(f, p, t, sec, 0)] += got(f, p, t, 1, sec)

    def fourth(t):
        for f in (1, 0):
            for p in range(2):
                receive(f, p, t, 2)
                put(f, p, t, 3, 0, pt[unit(f, p, t, NEXT[p], 0)] + got(f, p, t, 2, 1))
                send(f, p, t, 3)
                pt[unit(f, p, t, 0, 0)] += got(f, p, t, 2, 0)

    def fifth(t):
        for f in (1, 0):
            for p in range(2):
                receive(f, p, t, 3)
                pt[unit(f, p, t, 0, 0)] += got(f, p, t, 3, 0)
                for j, q in enumerate(FIRST[p]):

                    @pl.when(t == SLABS.index(q))
                    def _():
                        put(f, p, j, 4, 0, pt[unit(f, p, t, 0, 0)])
                        send(f, p, j, 4)

    def sixth():
        for f in (1, 0):
            for p in range(2):
                receive(f, p, 1, 4)
                put(f, p, 0, 5, 0, pt[unit(f, p, SLABS.index(NEXT[p]), 0, 0)] + got(f, p, 1, 4, 0))
                send(f, p, 0, 5)

    def last():
        for f in (1, 0):
            for p in range(2):
                for stage in (4, 5):
                    receive(f, p, 0, stage)
                    pt[unit(f, p, 3, 0, 0)] += got(f, p, 0, stage, 0)

    def step(t, carry):
        for k, stage in enumerate((first, second, third, fourth, fifth)):

            @pl.when(jnp.logical_and(t >= k, t < k + 4))
            def _():
                stage(t - k)

        @pl.when(t == 6)
        def _():
            sixth()

        return carry

    lax.fori_loop(0, 8, step, 0)
    last()
    for copy in inputs[1:]:
        copy.wait()

    def exact(l, r):
        return jnp.dot(l, r, preferred_element_type=F32, precision=lax.Precision.HIGHEST)

    accum = 0.9 * mom[0] + pt[3, 0, 0].T * (1.0 / math.sqrt(group_tok))
    mine = exact(exact(left[...], accum), right[...])
    band[...] = mine
    copies = [
        pltpu.make_async_remote_copy(
            band, bands.at[i - 1], band_ss.at[i - 1], band_rs.at[i - 1], device_id=((rep + i) % 4, own)
        )
        for i in (1, 2, 3)
    ]
    for copy in copies:
        copy.start()
    new[0] = accum - exact(exact(left_t[...], mine), right_t[...])
    outs = [pltpu.make_async_copy(*refs, out_sem.at[i]) for i, refs in enumerate(((up, up_hbm), (new, new_hbm)))]
    outs[1].start()
    for copy in copies:
        copy.wait_recv()
    mean = (mine + bands[0] + bands[1] + bands[2]) * 0.25
    up[...] = exact(exact(left_t[...], mean), right_t[...])
    outs[0].start()
    for copy in copies:
        copy.wait_send()
    pltpu.make_async_copy(sent, sent, sent_sem.at[0]).wait()
    for copy in outs:
        copy.wait()


def hand_on(up_ref, new_ref, up_out, new_out):
    up_out[...] = up_ref[...]
    new_out[...] = new_ref[...]


def shards(activations, cotangents, momentum):
    tok, d = activations.shape
    kw = cotangents.shape[1]
    basis = dct_basis()
    left = np.kron(np.eye(2, dtype=np.float32), basis)
    right = np.kron(np.eye(kw // 64, dtype=np.float32), basis.T)
    constants = [jnp.asarray(m) for m in (left, left.T.copy(), right, right.T.copy())]
    vmem = pl.BlockSpec(memory_space=pltpu.VMEM)
    hbm = pl.BlockSpec(memory_space=pl.ANY)
    dma = pltpu.SemaphoreType.DMA
    shapes = (jax.ShapeDtypeStruct((128, kw), F32), jax.ShapeDtypeStruct((1, 128, kw), F32))
    results = pl.pallas_call(
        functools.partial(kernel, tok * lax.axis_size("fsdp")),
        out_shape=shapes,
        in_specs=[hbm] * 7,
        out_specs=(hbm, hbm),
        scratch_shapes=[
            pltpu.VMEM((tok, d), BF16),
            pltpu.VMEM((tok, kw), BF16),
            pltpu.VMEM((kw, tok), BF16),
            pltpu.VMEM((1, 128, kw), F32),
            *[pltpu.VMEM(m.shape, F32) for m in constants],
            pltpu.VMEM((4, 4, 4, kw, 128), F32),
            pltpu.VMEM((4 * STARTS[6], 128), BF16),
            pltpu.VMEM((4 * STARTS[6], 128), BF16),
            pltpu.VMEM((2, 2, 16, 128), F32),
            pltpu.VMEM((2, 2, 16, 128), F32),
            *[pltpu.VMEM(m.shape, F32) for m in shapes],
            pltpu.VMEM((32, 128), F32),
            pltpu.VMEM((3, 32, 128), F32),
            dma((4, 4)),
            dma((6,)),
            dma((2,)),
            dma((1,)),
            dma((2, 2, 4, 6)),
            dma((3,)),
            dma((3,)),
        ],
        compiler_params=pltpu.CompilerParams(
            collective_id=0, has_side_effects=True, vmem_limit_bytes=60 * 2**20
        ),
        cost_estimate=pl.CostEstimate(flops=2 * tok * d * kw, bytes_accessed=2 * tok * (d + kw), transcendentals=0),
    )(activations, cotangents, momentum, *constants)
    return pl.pallas_call(
        hand_on,
        out_shape=shapes,
        in_specs=[vmem] * 2,
        out_specs=(vmem, vmem),
    )(*results)


def solution(mesh):
    return jax.shard_map(
        shards,
        mesh=mesh,
        in_specs=(P(("rep", "fsdp"), None), P(("rep", "fsdp"), None), P("rep", "fsdp", None)),
        out_specs=(P("fsdp", None), P("rep", "fsdp", None)),
        check_vma=False,
    )
```

time: 476 us -> 75.9 us (0.16)
  waiting for transfers between devices: 419 us -> 0 us
  Pallas kernels: 0 us -> 75.1 us
  blocking collectives: 19.2 us -> 0 us
  matrix products: 18.6 us -> 0 us
  between operations: 14.1 us -> 0.64 us
    reduce_scatter x1 -> x0, waiting for transfers between devices: 419 us -> none  [shards(): lax.psum_scatter(lax.dot_general(activations, cotangents, (((0,), (0,)),...]
    pallas_call x0 -> x2, Pallas kernels: none -> 75.1 us  [the longest x1 73.3 us: shards(): pl.pallas_call(functools.partial(kernel, tok * lax.axis_size('fsdp')), ou...]
    all_gather x1 -> x0, blocking collectives: 19.2 us -> none  [shards(): every_band = lax.all_gather(own_band[None], 'rep', axis=0, tiled=True)]
    dot_general x7 -> x0, matrix products: 18.6 us -> none  [the longest x1 15 us: shards(): lax.dot_general(activations, cotangents, (((0,), (0,)), ((), ())), prefer...]
  transfers between devices with their start and end apart: 1 -> 0, of which waited for: 1 -> 0; matrix products, arithmetic and copies ran while one was open for 0% -> 0% of each run, Pallas kernels for 0% -> 0%
where the time goes in v2:
time: 75.9 us; the launch traced here: 75.8 us
  Pallas kernels  75.1 us (99%)
    pallas_call x1, Pallas kernels, shards(): pl.pallas_call(functools.partial(kernel, tok * lax.axis_size('fsdp')), ou...  73.3 us
    pallas_call x1, Pallas kernels, shards(): pl.pallas_call(hand_on, out_shape=shapes, in_specs=[vmem] * 2, out_specs=...  1.84 us

profile of v2, /device:TPU:1, one launch (start us, length us, event | category | flops | bytes accessed | tf_op | source)
XLA Modules:
  0.0 75.8 jit_solution(9537469938919749431)
XLA Ops:
  0.6 73.3 %shard_map.86 = (f32[128,512]{1,0:T(8,128)}, f32[1,128,512]{2,1,0:T(8,128)}) custom-call(bf16[768,8192]{1,0:T(8,128)(2,1)} %a_hbm.1, bf16[768,512]{1,0:T(8,128)(2,1)} %c_hbm.1, f32[1,128,512]{2,1,0:T(8,128)} %mom_hbm.1, f32[32,128]{1,0:T(8,128)} %constant.8.clone.left_hbm, f32[128,32]{1,0:T(8,128)} %constant.9.clone.left_t_hbm, ...), custom_call_target="tpu_custom_call" | custom-call | flops 6442450944 | bytes 13369344 | tf_op jit(solution)/shard_map/pallas_call | solution.py:282
  73.9 1.8 %shard_map.87 = (f32[128,512]{1,0:T(8,128)}, f32[1,128,512]{2,1,0:T(8,128)}) custom-call(f32[128,512]{1,0:T(8,128)} %get-tuple-element.4.up_ref, f32[1,128,512]{2,1,0:T(8,128)} %get-tuple-element.5.new_ref), custom_call_target="tpu_custom_call" | custom-call | tf_op jit(solution)/shard_map/pallas_call | solution.py:314

commit v3 on v2

--- a/solution.py
+++ b/solution.py
@@ -14,10 +14,16 @@
 FIRST = ((1, 2), (3, 2))
 NEXT = (3, 1)
 SLABS = (2, 1, 3, 0)
-UNITS = (8, 4, 2, 1, 1, 1)
-COUNTS = (4, 4, 4, 4, 2, 1)
-SIZES = tuple(n * 128 + 16 for n in UNITS)
-STARTS = tuple(sum(n * m for n, m in zip(SIZES[:i], COUNTS)) for i in range(7))
+PORTIONS = ((1, 0), (1, 1), (0, 0), (0, 1))
+DEPTH = (112, 112, 32)
+UNITS = ((8, 4, 2, 1, 1, 1),) * 2 + ((8, 4, 4, 1),)
+COUNTS = ((4, 4, 2, 2, 3, 6),) * 2 + ((4, 4, 3, 3),)
+SIZES = tuple(tuple(n * depth + 16 for n in units) for depth, units in zip(DEPTH, UNITS))
+STARTS = tuple(
+    tuple(sum(n * m for n, m in zip(sizes[:i], counts)) for i in range(len(sizes) + 1))
+    for sizes, counts in zip(SIZES, COUNTS)
+)
+FAMILIES = tuple(2 * sum(starts[-1] for starts in STARTS[:i]) for i in range(4))
 SPAN = 250.0
 
 
@@ -73,7 +79,7 @@
         return pltpu.make_async_copy(a_hbm.at[:, cols], a.at[:, cols], a_sem.at[t, ry])
 
     barrier = pltpu.get_barrier_semaphore()
-    others = [partner(axis, mask) for axis in "xyz" for mask in (1, 3)]
+    others = [partner(axis, mask) for axis in "xyz" for mask in (1, 2, 3)]
     others += [((rep + i) % 4, own) for i in (1, 2, 3)]
     for other in others:
         pl.semaphore_signal(barrier, inc=1, device_id=other)
@@ -89,42 +95,42 @@
     ct[...] = c[...].T
     ssc[...] = jnp.zeros_like(ssc)
 
-    def axis_of(f, stage):
-        return ("xxyyzz", "yyxxzz")[f][stage]
+    def axis_of(f, p, stage):
+        return ("zzxy", "zzyx")[p][stage] if f == 2 else ("xxyyzy", "yyxxzx")[f][stage]
 
     def mask_of(p, stage):
         return (FIRST[p][0], NEXT[p])[stage % 2]
 
     def begin(f, p, t, stage, row=0):
-        at = (f * 2 + p) * STARTS[6] + STARTS[stage] + t * SIZES[stage] + row
+        at = FAMILIES[f] + p * STARTS[f][-1] + STARTS[f][stage] + t * SIZES[f][stage] + row
         return at if isinstance(at, int) else pl.multiple_of(at, 16)
 
-    def message(f, p, t, stage):
-        where = pl.ds(begin(f, p, t, stage), SIZES[stage])
+    def message(f, p, t, stage, mask=None):
+        where = pl.ds(begin(f, p, t, stage), SIZES[f][stage])
         return pltpu.make_async_remote_copy(
             sent.at[where], received.at[where], sent_sem.at[0], rs.at[f, p, t, stage],
-            device_id=partner(axis_of(f, stage), mask_of(p, stage)),
+            device_id=partner(axis_of(f, p, stage), mask or mask_of(p, stage)),
         )
 
     def put(f, p, t, stage, row, v):
         code, s = encode(v)
-        sent[pl.ds(begin(f, p, t, stage, row * 128), 128), :] = code
+        sent[pl.ds(begin(f, p, t, stage, row * DEPTH[f]), DEPTH[f]), :] = code
         ssc[f, p, pl.ds(row, 1), :] = s
 
-    def send(f, p, t, stage):
-        sent[pl.ds(begin(f, p, t, stage, UNITS[stage] * 128), 16), :] = ssc[f, p].astype(BF16)
-        message(f, p, t, stage).start()
+    def send(f, p, t, stage, mask=None):
+        sent[pl.ds(begin(f, p, t, stage, UNITS[f][stage] * DEPTH[f]), 16), :] = ssc[f, p].astype(BF16)
+        message(f, p, t, stage, mask).start()
 
     def receive(f, p, t, stage):
         message(f, p, t, stage).wait_recv()
-        rsc[f, p] = received[pl.ds(begin(f, p, t, stage, UNITS[stage] * 128), 16), :].astype(F32)
+        rsc[f, p] = received[pl.ds(begin(f, p, t, stage, UNITS[f][stage] * DEPTH[f]), 16), :].astype(F32)
 
     def got(f, p, t, stage, row):
-        return decode(received[pl.ds(begin(f, p, t, stage, row * 128), 128), :], rsc[f, p, pl.ds(row, 1), :])
+        return decode(received[pl.ds(begin(f, p, t, stage, row * DEPTH[f]), DEPTH[f]), :], rsc[f, p, pl.ds(row, 1), :])
 
     def unit(f, p, t, sec, pri):
         at = (sec, pri) if f == 0 else (pri, sec)
-        return (t,) + at + (slice((f * 2 + p) * 128, (f * 2 + p) * 128 + 128), slice(None))
+        return (t,) + at + (slice((f * 2 + p) * 112, (f * 2 + p) * 112 + 112), slice(None))
 
     def multiply(t, ry):
         zh = flip(z0, slab(t))
@@ -137,100 +143,185 @@
         for rx in range(4):
             pt[t, ry, rx] = total[:, rx * 128 : rx * 128 + 128]
 
-    def first(t):
+    def z_unit(p, rz, ry, rx):
+        return (SLABS.index(rz), ry, rx, slice(448 + p * 32, 480 + p * 32), slice(None))
+
+    def products(t):
         for ry in SLABS:
             multiply(t, ry)
-            for p in range(2):
-                for j, rx in enumerate(FIRST[p]):
-                    put(0, p, t, 0, j * 4 + ry, pt[unit(0, p, t, ry, rx)])
-            for p in range(2):
-                if ry in FIRST[p]:
+
+    def first(t):
+        @pl.when(t == 0)
+        def _():
+            pl.semaphore_wait(barrier, len(others))
+
+        for f, p in PORTIONS:
+            for j, pri in enumerate(FIRST[p]):
+                for sec in range(4):
+                    put(f, p, t, 0, j * 4 + sec, pt[unit(f, p, t, sec, pri)])
+            send(f, p, t, 0)
+
+    def z_first():
+        for p in range(2):
+
+            def one(ry, carry):
+                for j, rz in enumerate(FIRST[p]):
                     for rx in range(4):
-                        put(1, p, t, 0, FIRST[p].index(ry) * 4 + rx, pt[unit(1, p, t, rx, ry)])
-            if ry == 1:
-
-                @pl.when(t == 0)
+                        put(2, p, ry, 0, j * 4 + rx, pt[z_unit(p, rz, ry, rx)])
+                send(2, p, ry, 0)
+                return carry
+
+            lax.fori_loop(0, 4, one, 0)
+
+    def z_second():
+        for p in range(2):
+
+            def one(ry, carry):
+                receive(2, p, ry, 0)
+                for rx in range(4):
+                    put(2, p, ry, 1, rx, pt[z_unit(p, NEXT[p], ry, rx)] + got(2, p, ry, 0, 4 + rx))
+                send(2, p, ry, 1)
+                for rx in range(4):
+                    pt[z_unit(p, 0, ry, rx)] += got(2, p, ry, 0, rx)
+                return carry
+
+            lax.fori_loop(0, 4, one, 0)
+
+    def z_third():
+        for p in range(2):
+
+            def one(ry, carry):
+                receive(2, p, ry, 1)
+                for rx in range(4):
+                    pt[z_unit(p, 0, ry, rx)] += got(2, p, ry, 1, rx)
+                return carry
+
+            lax.fori_loop(0, 4, one, 0)
+            for m in (2, 1, 3):
+                for other in range(4):
+                    ry, rx = (other, m) if p == 0 else (m, other)
+                    put(2, p, m - 1, 2, other, pt[z_unit(p, 0, ry, rx)])
+                send(2, p, m - 1, 2, m)
+
+    def z_fourth():
+        for p in range(2):
+            for m in (1, 3, 2):
+                receive(2, p, m - 1, 2)
+                for other in range(4):
+                    ry, rx = (other, 0) if p == 0 else (0, other)
+                    pt[z_unit(p, 0, ry, rx)] += got(2, p, m - 1, 2, other)
+            for m in (2, 1, 3):
+                ry, rx = (m, 0) if p == 0 else (0, m)
+                put(2, p, m - 1, 3, 0, pt[z_unit(p, 0, ry, rx)])
+                send(2, p, m - 1, 3, m)
+
+    def z_last():
+        for p in range(2):
+            for m in (1, 3, 2):
+                receive(2, p, m - 1, 3)
+                pt[z_unit(p, 0, 0, 0)] += got(2, p, m - 1, 3, 0)
+
+    def second(t):
+        for f, p in PORTIONS:
+            receive(f, p, t, 0)
+
+            def pass_on(sec, carry):
+                put(f, p, t, 1, sec, pt[unit(f, p, t, sec, NEXT[p])] + got(f, p, t, 0, 4 + sec))
+                return carry
+
+            lax.fori_loop(0, 4, pass_on, 0)
+            send(f, p, t, 1)
+        for f, p in PORTIONS:
+
+            def keep(sec, carry):
+                pt[unit(f, p, t, sec, 0)] += got(f, p, t, 0, sec)
+                return carry
+
+            lax.fori_loop(0, 4, keep, 0)
+
+    def third_pairs(t):
+        for f, p in PORTIONS:
+            receive(f, p, t, 1)
+            for j, sec in enumerate(FIRST[p]):
+                put(f, p, t, 2, j, pt[unit(f, p, t, sec, 0)] + got(f, p, t, 1, sec))
+            send(f, p, t, 2)
+        for f, p in PORTIONS:
+            for sec in (0, NEXT[p]):
+                pt[unit(f, p, t, sec, 0)] += got(f, p, t, 1, sec)
+
+    def third_direct(t):
+        for f, p in PORTIONS:
+            receive(f, p, t, 1)
+            for m in (2, 1, 3):
+                slot = (t - 2) * 3 + m - 1
+                put(f, p, slot, 5, 0, pt[unit(f, p, t, m, 0)] + got(f, p, t, 1, m))
+                send(f, p, slot, 5, m)
+        for f, p in PORTIONS:
+            pt[unit(f, p, t, 0, 0)] += got(f, p, t, 1, 0)
+
+    def fourth_pairs(t):
+        for f, p in PORTIONS:
+            receive(f, p, t, 2)
+            put(f, p, t, 3, 0, pt[unit(f, p, t, NEXT[p], 0)] + got(f, p, t, 2, 1))
+            send(f, p, t, 3)
+        for f, p in PORTIONS:
+            pt[unit(f, p, t, 0, 0)] += got(f, p, t, 2, 0)
+
+    def fourth_direct(t):
+        for f, p in PORTIONS:
+            v = pt[unit(f, p, t, 0, 0)]
+            for m in (1, 3, 2):
+                slot = (t - 2) * 3 + m - 1
+                receive(f, p, slot, 5)
+                v += got(f, p, slot, 5, 0)
+            pt[unit(f, p, t, 0, 0)] = v
+
+            @pl.when(t == 2)
+            def _():
+                put(f, p, 2, 4, 0, pt[unit(f, p, t, 0, 0)])
+                send(f, p, 2, 4, 3)
+
+    def fifth(t):
+        for f, p in PORTIONS:
+            receive(f, p, t, 3)
+            pt[unit(f, p, t, 0, 0)] += got(f, p, t, 3, 0)
+            for q in (2, 1):
+
+                @pl.when(t == SLABS.index(q))
                 def _():
-                    pl.semaphore_wait(barrier, len(others))
-
-                send(1, 0, t, 0)
-            if ry == 3:
-                send(1, 1, t, 0)
-        send(0, 0, t, 0)
-        send(0, 1, t, 0)
-
-    def second(t):
-        for f in (1, 0):
-            for p in range(2):
-                receive(f, p, t, 0)
-
-                def one(sec, carry):
-                    put(f, p, t, 1, sec, pt[unit(f, p, t, sec, NEXT[p])] + got(f, p, t, 0, 4 + sec))
-                    pt[unit(f, p, t, sec, 0)] += got(f, p, t, 0, sec)
-                    return carry
-
-                lax.fori_loop(0, 4, one, 0)
-                send(f, p, t, 1)
-
-    def third(t):
-        for f in (1, 0):
-            for p in range(2):
-                receive(f, p, t, 1)
-                for j, sec in enumerate(FIRST[p]):
-                    put(f, p, t, 2, j, pt[unit(f, p, t, sec, 0)] + got(f, p, t, 1, sec))
-                send(f, p, t, 2)
-                for sec in (0, NEXT[p]):
-                    pt[unit(f, p, t, sec, 0)] += got(f, p, t, 1, sec)
-
-    def fourth(t):
-        for f in (1, 0):
-            for p in range(2):
-                receive(f, p, t, 2)
-                put(f, p, t, 3, 0, pt[unit(f, p, t, NEXT[p], 0)] + got(f, p, t, 2, 1))
-                send(f, p, t, 3)
-                pt[unit(f, p, t, 0, 0)] += got(f, p, t, 2, 0)
-
-    def fifth(t):
-        for f in (1, 0):
-            for p in range(2):
-                receive(f, p, t, 3)
-                pt[unit(f, p, t, 0, 0)] += got(f, p, t, 3, 0)
-                for j, q in enumerate(FIRST[p]):
-
-                    @pl.when(t == SLABS.index(q))
-                    def _():
-                        put(f, p, j, 4, 0, pt[unit(f, p, t, 0, 0)])
-                        send(f, p, j, 4)
-
-    def sixth():
-        for f in (1, 0):
-            for p in range(2):
-                receive(f, p, 1, 4)
-                put(f, p, 0, 5, 0, pt[unit(f, p, SLABS.index(NEXT[p]), 0, 0)] + got(f, p, 1, 4, 0))
-                send(f, p, 0, 5)
-
-    def last():
-        for f in (1, 0):
-            for p in range(2):
-                for stage in (4, 5):
-                    receive(f, p, 0, stage)
-                    pt[unit(f, p, 3, 0, 0)] += got(f, p, 0, stage, 0)
+                    put(f, p, q - 1, 4, 0, pt[unit(f, p, t, 0, 0)])
+                    send(f, p, q - 1, 4, q)
+
+    def last(q):
+        for f, p in PORTIONS:
+            receive(f, p, q - 1, 4)
+            pt[unit(f, p, 3, 0, 0)] += got(f, p, q - 1, 4, 0)
+
+    def at(when, stage, t):
+        pl.when(when)(lambda: stage(t))
 
     def step(t, carry):
-        for k, stage in enumerate((first, second, third, fourth, fifth)):
-
-            @pl.when(jnp.logical_and(t >= k, t < k + 4))
-            def _():
-                stage(t - k)
-
-        @pl.when(t == 6)
-        def _():
-            sixth()
-
+        at(t < 4, first, t)
+        at(t < 3, products, t + 1)
+        pl.when(t == 2)(z_first)
+        at(jnp.logical_and(t >= 1, t < 5), second, t - 1)
+        at(jnp.logical_and(t >= 2, t < 4), third_pairs, t - 2)
+        at(t >= 4, third_direct, t - 2)
+        at(jnp.logical_and(t >= 3, t < 5), fourth_pairs, t - 3)
+        pl.when(t == 3)(z_second)
+        pl.when(t == 4)(z_third)
+        pl.when(t == 5)(z_fourth)
+        at(t >= 5, fourth_direct, t - 3)
+        at(t >= 4, fifth, t - 4)
         return carry
 
-    lax.fori_loop(0, 8, step, 0)
-    last()
+    products(0)
+    lax.fori_loop(0, 6, step, 0)
+    last(2)
+    last(1)
+    fourth_direct(3)
+    z_last()
+    last(3)
     for copy in inputs[1:]:
         copy.wait()
 
@@ -291,10 +382,10 @@
             pltpu.VMEM((1, 128, kw), F32),
             *[pltpu.VMEM(m.shape, F32) for m in constants],
             pltpu.VMEM((4, 4, 4, kw, 128), F32),
-            pltpu.VMEM((4 * STARTS[6], 128), BF16),
-            pltpu.VMEM((4 * STARTS[6], 128), BF16),
-            pltpu.VMEM((2, 2, 16, 128), F32),
-            pltpu.VMEM((2, 2, 16, 128), F32),
+            pltpu.VMEM((FAMILIES[3], 128), BF16),
+            pltpu.VMEM((FAMILIES[3], 128), BF16),
+            pltpu.VMEM((3, 2, 16, 128), F32),
+            pltpu.VMEM((3, 2, 16, 128), F32),
             *[pltpu.VMEM(m.shape, F32) for m in shapes],
             pltpu.VMEM((32, 128), F32),
             pltpu.VMEM((3, 32, 128), F32),
@@ -302,7 +393,7 @@
             dma((6,)),
             dma((2,)),
             dma((1,)),
-            dma((2, 2, 4, 6)),
+            dma((3, 2, 6, 6)),
             dma((3,)),
             dma((3,)),
         ],

time: 75.9 us -> 72.3 us (0.953)
  Pallas kernels: 75.1 us -> 71.5 us
    pallas_call x1, Pallas kernels: 73.3 us -> 69.7 us  [shards(): pl.pallas_call(functools.partial(kernel, tok * lax.axis_size('fsdp')), ou...]
where the time goes in v3:
time: 72.3 us; the launch traced here: 72.2 us
  Pallas kernels  71.5 us (99%)
    pallas_call x1, Pallas kernels, shards(): pl.pallas_call(functools.partial(kernel, tok * lax.axis_size('fsdp')), ou...  69.7 us
    pallas_call x1, Pallas kernels, shards(): pl.pallas_call(hand_on, out_shape=shapes, in_specs=[vmem] * 2, out_specs=...  1.84 us

profile of v3, /device:TPU:1, one launch (start us, length us, event | category | flops | bytes accessed | tf_op | source)
XLA Modules:
  0.0 72.2 jit_solution(1286000174077224892)
XLA Ops:
  0.6 69.7 %shard_map.86 = (f32[128,512]{1,0:T(8,128)}, f32[1,128,512]{2,1,0:T(8,128)}) custom-call(bf16[768,8192]{1,0:T(8,128)(2,1)} %a_hbm.1, bf16[768,512]{1,0:T(8,128)(2,1)} %c_hbm.1, f32[1,128,512]{2,1,0:T(8,128)} %mom_hbm.1, f32[32,128]{1,0:T(8,128)} %constant.8.clone.left_hbm, f32[128,32]{1,0:T(8,128)} %constant.9.clone.left_t_hbm, ...), custom_call_target="tpu_custom_call" | custom-call | flops 6442450944 | bytes 13369344 | tf_op jit(solution)/shard_map/pallas_call | solution.py:373
  70.3 1.8 %shard_map.87 = (f32[128,512]{1,0:T(8,128)}, f32[1,128,512]{2,1,0:T(8,128)}) custom-call(f32[128,512]{1,0:T(8,128)} %get-tuple-element.4.up_ref, f32[1,128,512]{2,1,0:T(8,128)} %get-tuple-element.5.new_ref), custom_call_target="tpu_custom_call" | custom-call | tf_op jit(solution)/shard_map/pallas_call | solution.py:405

commit v4 on v3

--- a/solution.py
+++ b/solution.py
@@ -305,12 +305,12 @@
         at(t < 3, products, t + 1)
         pl.when(t == 2)(z_first)
         at(jnp.logical_and(t >= 1, t < 5), second, t - 1)
+        pl.when(t == 3)(z_second)
+        pl.when(t == 5)(z_fourth)
+        pl.when(t == 4)(z_third)
         at(jnp.logical_and(t >= 2, t < 4), third_pairs, t - 2)
         at(t >= 4, third_direct, t - 2)
         at(jnp.logical_and(t >= 3, t < 5), fourth_pairs, t - 3)
-        pl.when(t == 3)(z_second)
-        pl.when(t == 4)(z_third)
-        pl.when(t == 5)(z_fourth)
         at(t >= 5, fourth_direct, t - 3)
         at(t >= 4, fifth, t - 4)
         return carry

time: 72.3 us -> 71.6 us (level)
  no operation moved by 1% of the time
where the time goes in v4:
time: 71.6 us; the launch traced here: 71.5 us
  Pallas kernels  70.8 us (99%)
    pallas_call x1, Pallas kernels, shards(): pl.pallas_call(functools.partial(kernel, tok * lax.axis_size('fsdp')), ou...  69 us
    pallas_call x1, Pallas kernels, shards(): pl.pallas_call(hand_on, out_shape=shapes, in_specs=[vmem] * 2, out_specs=...  1.84 us

profile of v4, /device:TPU:1, one launch (start us, length us, event | category | flops | bytes accessed | tf_op | source)
XLA Modules:
  0.0 71.5 jit_solution(11371799575690329321)
XLA Ops:
  0.6 69.0 %shard_map.86 = (f32[128,512]{1,0:T(8,128)}, f32[1,128,512]{2,1,0:T(8,128)}) custom-call(bf16[768,8192]{1,0:T(8,128)(2,1)} %a_hbm.1, bf16[768,512]{1,0:T(8,128)(2,1)} %c_hbm.1, f32[1,128,512]{2,1,0:T(8,128)} %mom_hbm.1, f32[32,128]{1,0:T(8,128)} %constant.8.clone.left_hbm, f32[128,32]{1,0:T(8,128)} %constant.9.clone.left_t_hbm, ...), custom_call_target="tpu_custom_call" | custom-call | flops 6442450944 | bytes 13369344 | tf_op jit(solution)/shard_map/pallas_call | solution.py:373
  69.6 1.8 %shard_map.87 = (f32[128,512]{1,0:T(8,128)}, f32[1,128,512]{2,1,0:T(8,128)}) custom-call(f32[128,512]{1,0:T(8,128)} %get-tuple-element.4.up_ref, f32[1,128,512]{2,1,0:T(8,128)} %get-tuple-element.5.new_ref), custom_call_target="tpu_custom_call" | custom-call | tf_op jit(solution)/shard_map/pallas_call | solution.py:405
